TPU v7x, 32 devices: a whole 2x2x4 slice. The times are simulated.
32 devices in a mesh: box: 16 (over z, y, core), angle: 2 (over x).
Axes of the slice: x: 2, y: 2, z: 4, core: 2. Of those that a mesh axis runs over, the one named last changes fastest.
Arguments:
- child_field: bfloat16 [1024, 2, 64, 128], P('box', None, 'angle'), may hold values from -6 to 6
- child_list: int32 [1024, 8], P('box'), may hold values from -1 to 1023, as said below
- child_op: int32 [1024, 8], P('box'), may hold values from 0 to 39
- child_home: int32 [1024], replicated, may hold values from 0 to 1023, as said below
- child_ops: bfloat16 [40, 2, 64, 128], P(None, None, 'angle'), may hold values from -2 to 2
- parent_list: int32 [256, 8], P('box'), may hold values from -1 to 255, as said below
- parent_op: int32 [256, 8], P('box'), may hold values from 0 to 39
- parent_home: int32 [256], replicated, may hold values from 0 to 255, as said below
- parent_ops: bfloat16 [40, 2, 128, 256], P(None, None, 'angle'), may hold values from -2 to 2
Outputs:
- child_out: bfloat16 [1024, 2, 64, 128], P('box', None, 'angle')
Inputs may be any that keep to these rules, and one draw needn't show every extreme that they name: `child_list`: entries are child box ids, or -1 for an empty slot. Among the list rows held by one index of box, at most 32 entries name boxes whose row child_home lies on one index of box (row // 64); some pair of indices reaches 32 in every draw. Entries may repeat. A permutation: child box i is held in row child_home[i]. `parent_list`: entries are parent box ids, or -1 for an empty slot. Among the list rows held by one index of box, at most 8 entries name boxes whose row parent_home lies on one index of box (row // 16); some pair of indices reaches 8 in every draw. Entries may repeat. A permutation: parent box i is held in row parent_home[i].
All inputs are finite; a program needn't handle non-finite values.
Results may differ from a plain program's by a relative error of at most 0.0017.
The roundings to bfloat16 on the way count: a program that leaves them out, or rounds other values in their place, can miss the bound.
Values may be sent and summed in bfloat16 or wider, within the bound.
A program may use at most 128 MiB of HBM per device.

v0:
```python
import math

import jax
import jax.numpy as jnp
from jax import lax
from jax.sharding import PartitionSpec as P

CT = 64
SUBBOX_HEADINGS = 128
PT = 128
PP = 256
KIDS = 4


WAVE_NUMBER = 6.0


def fourier_table(fine_count, coarse_count, offset):
    fine_pos = (jnp.arange(fine_count, dtype=jnp.float32) + offset) / fine_count
    coarse_pos = (jnp.arange(coarse_count, dtype=jnp.float32) + offset) / coarse_count
    distance = fine_pos[:, None] - coarse_pos[None, :]
    harmonic = jnp.arange(1, coarse_count // 2, dtype=jnp.float32)
    cosines = jnp.cos(2.0 * math.pi * harmonic[None, None, :] * distance[:, :, None])
    summed = 1.0 + 2.0 * jnp.sum(cosines, axis=2) + jnp.cos(math.pi * coarse_count * distance)
    return summed / coarse_count


def shift_parts(polar_rows):
    polar_angle = math.pi * (polar_rows.astype(jnp.float32) + 0.5) / PT
    heading_radians = 2.0 * math.pi / PP * jnp.arange(PP, dtype=jnp.float32)
    kid_index = jnp.arange(KIDS, dtype=jnp.int32)
    side_x = (2 * (kid_index % 2) - 1).astype(jnp.float32)
    side_y = (2 * (kid_index // 2 % 2) - 1).astype(jnp.float32)
    across = (
        side_x[:, None] * jnp.cos(heading_radians)[None, :]
        + side_y[:, None] * jnp.sin(heading_radians)[None, :]
    )
    phase_arg = WAVE_NUMBER * jnp.sin(polar_angle)[None, :, None] * across[:, None, :]
    return (jnp.cos(phase_arg), jnp.sin(phase_arg))


def lift_sum(widened, cos_part, sin_part):
    real_part = jnp.sum(
        cos_part * widened[..., 0, :, :] - sin_part * widened[..., 1, :, :], axis=-3
    )
    imag_part = jnp.sum(
        cos_part * widened[..., 1, :, :] + sin_part * widened[..., 0, :, :], axis=-3
    )
    return jnp.stack([real_part, imag_part], axis=-3).astype(jnp.bfloat16)


def lower_turn(parents, cos_part, sin_part):
    real_in = jnp.expand_dims(parents[..., 0, :, :].astype(jnp.float32), -3)
    imag_in = jnp.expand_dims(parents[..., 1, :, :].astype(jnp.float32), -3)
    real_out = cos_part * real_in + sin_part * imag_in
    imag_out = cos_part * imag_in - sin_part * real_in
    return jnp.stack([real_out, imag_out], axis=-3).astype(jnp.bfloat16)


def plan_requests(far_lists, home_rows, rows_device, owners):
    flat_ids = far_lists.reshape(-1)
    usable = flat_ids >= 0
    target_row = home_rows[jnp.where(usable, flat_ids, 0)]
    owner_of = target_row // rows_device
    local_row = target_row - owner_of * rows_device
    capacity = flat_ids.shape[0] // owners
    matches = (
        (owner_of[:, None] == jnp.arange(owners, dtype=jnp.int32)[None, :]) & usable[:, None]
    ).astype(jnp.int32)
    earlier = jnp.cumsum(matches, axis=0) - matches
    rank_in = jnp.sum(earlier * matches, axis=1)
    position = jnp.where(usable, owner_of * capacity + rank_in, owners * capacity)
    wanted = jnp.zeros((owners * capacity,), jnp.int32).at[position].set(local_row, mode="drop")
    return (wanted.reshape(owners, capacity), position, usable)


def translate_sum(received, position, usable, op_index, op_table):
    rows_here, slot_count = op_index.shape
    pattern_shape = received.shape[2:]
    flat_in = received.reshape((-1,) + pattern_shape)
    clipped = jnp.minimum(position, flat_in.shape[0] - 1)
    source = flat_in[clipped].reshape((rows_here, slot_count) + pattern_shape)
    translator = op_table[op_index]
    weight = usable.reshape(rows_here, slot_count, 1, 1).astype(jnp.float32)
    src_real = source[:, :, 0].astype(jnp.float32)
    src_imag = source[:, :, 1].astype(jnp.float32)
    op_real = translator[:, :, 0].astype(jnp.float32)
    op_imag = translator[:, :, 1].astype(jnp.float32)
    real_part = jnp.sum(weight * (op_real * src_real - op_imag * src_imag), axis=1)
    imag_part = jnp.sum(weight * (op_real * src_imag + op_imag * src_real), axis=1)
    return jnp.stack([real_part, imag_part], axis=1)


def local(
    child_field,
    child_list,
    child_op,
    child_home,
    child_ops,
    parent_list,
    parent_op,
    parent_home,
    parent_ops,
):
    owners = lax.axis_size("box")
    angle_index = lax.axis_index("angle")
    child_rows = child_field.shape[0]
    parent_rows = parent_list.shape[0]
    child_thin = child_field.shape[2]
    parent_thin = parent_ops.shape[2]
    child_wanted, child_position, child_usable = plan_requests(
        child_list, child_home, child_rows, owners
    )
    parent_wanted, parent_position, parent_usable = plan_requests(
        parent_list, parent_home, parent_rows, owners
    )
    child_asked, parent_asked = (
        lax.all_to_all(child_wanted, "box", split_axis=0, concat_axis=0, tiled=True),
        lax.all_to_all(parent_wanted, "box", split_axis=0, concat_axis=0, tiled=True),
    )
    child_sent = lax.all_to_all(
        child_field[child_asked], "box", split_axis=0, concat_axis=0, tiled=True
    )
    child_far = translate_sum(child_sent, child_position, child_usable, child_op, child_ops)
    theta_up = fourier_table(PT, CT, 0.5).astype(jnp.bfloat16)
    phi_up = fourier_table(PP, SUBBOX_HEADINGS, 0.0).T.astype(jnp.bfloat16)
    theta_down = (fourier_table(PT, CT, 0.5).T * (CT / PT)).astype(jnp.bfloat16)
    phi_down = (fourier_table(PP, SUBBOX_HEADINGS, 0.0) * (SUBBOX_HEADINGS / PP)).astype(
        jnp.bfloat16
    )
    up_rows = lax.dynamic_slice_in_dim(theta_up, angle_index * parent_thin, parent_thin, 0)
    columns = up_rows
    stretched = jnp.einsum(
        "ut,rctp->rcup",
        columns,
        lax.all_gather(child_field, "angle", axis=2, tiled=True),
        preferred_element_type=jnp.float32,
    ).astype(jnp.bfloat16)
    widened = jnp.einsum("rcup,pv->rcuv", stretched, phi_up, preferred_element_type=jnp.float32)
    local_polar = angle_index * parent_thin + jnp.arange(parent_thin, dtype=jnp.int32)
    cos_local, sin_local = shift_parts(local_polar)
    parent_field = lift_sum(
        widened.reshape(parent_rows, KIDS, 2, parent_thin, PP), cos_local, sin_local
    )
    parent_sent = lax.all_to_all(
        parent_field[parent_asked], "box", split_axis=0, concat_axis=0, tiled=True
    )
    parent_far = translate_sum(
        parent_sent, parent_position, parent_usable, parent_op, parent_ops
    ).astype(jnp.bfloat16)
    down_rows = lax.dynamic_slice_in_dim(theta_down, angle_index * child_thin, child_thin, 0)
    block_piece = lax.all_gather(parent_far, "angle", axis=2, tiled=True)
    span_rows = block_piece.shape[2]
    cos_piece, sin_piece = shift_parts(jnp.arange(span_rows, dtype=jnp.int32))
    turned = lower_turn(block_piece, cos_piece, sin_piece)
    narrowed = jnp.einsum(
        "qkcuv,vp->qkcup", turned, phi_down, preferred_element_type=jnp.float32
    ).astype(jnp.bfloat16)
    columns = down_rows
    summed_term = jnp.einsum(
        "tu,qkcup->qkctp", columns, narrowed, preferred_element_type=jnp.float32
    )
    child_term = summed_term.astype(jnp.bfloat16).reshape(
        child_rows, 2, child_thin, SUBBOX_HEADINGS
    )
    child_term = lax.optimization_barrier(child_term)
    return (child_far + child_term.astype(jnp.float32)).astype(jnp.bfloat16)


def solution(mesh):
    return jax.shard_map(
        local,
        mesh=mesh,
        in_specs=(
            P("box", None, "angle", None),
            P("box", None),
            P("box", None),
            P(),
            P(None, None, "angle", None),
            P("box", None),
            P("box", None),
            P(),
            P(None, None, "angle", None),
        ),
        out_specs=P("box", None, "angle", None),
        check_vma=False,
    )
```

profile of v0, /device:TPU:18, one launch (start us, length us, event | category | flops | bytes accessed | tf_op | source)
XLA Modules:
  0.0 522.8 jit_solution(13120406909631200074)
XLA Ops:
  7.3 0.8 copy.131
  8.9 1.6 gather_fusion.5
  11.2 1.0 scatter_custom_fusion.1
  12.9 6.2 %all-to-all-start.2 = ((s32[16,1,8]{2,1,0:T(1,128)}), s32[16,1,8]{2,1,0:T(1,128)S(1)}, u32[]{:S(2)}, u32[]{:S(2)}) async-start(s32[16,1,8]{2,1,0:T(1,128)} %bitcast.33), calls=%async_computation.2 | async-start | bytes 16384 | tf_op jit(solution)/shard_map/all_to_all | solution.py:119
  20.8 3.4 gather_fusion.1
  24.5 1.2 reduce-window.6
  26.1 3.3 cosine_reduce_fusion.1
  29.7 1.0 multiply_cosine_fusion.1
  30.7 27.4 %cosine_reduce_fusion = f32[256,128]{1,0:T(8,128)S(1)} fusion(f32[256,128]{1,0:T(8,128)S(1)} %broadcast_subtract_fusion, f32[63]{0:T(128)S(1)} %add_multiply_fusion), kind=kLoop, calls=%fused_computation.46 | loop fusion | flops 4096000 | bytes 262396 | tf_op jit(solution)/shard_map/reduce_sum | solution.py:24
  58.2 2.9 scatter_custom_fusion
  61.7 6.0 %all-to-all-start = ((s32[16,1,32]{2,1,0:T(1,128)}), s32[16,1,32]{2,1,0:T(1,128)S(1)}, u32[]{:S(2)}, u32[]{:S(2)}) async-start(s32[16,1,32]{2,1,0:T(1,128)} %all_to_all.22), calls=%async_computation | async-start | bytes 16384 | tf_op jit(solution)/shard_map/all_to_all | solution.py:118
  68.0 7.2 %fusion.29 = f32[64,2,64,256]{3,2,1,0:T(8,128)} fusion(bf16[64,2,64,128]{3,2,1,0:T(8,128)(2,1)} %all-gather.3.cloned.1.call-done, f32[256,128]{1,0:T(8,128)S(1)} %cosine_reduce_fusion, f32[128]{0:T(128)S(1)} %get-tuple-element.37, f32[256]{0:T(256)S(1)} %iota_multiply_fusion, f32[128,64]{0,1:T(8,128)S(1)} %broadcast_subtract_fusion.3, s32[]{:T(128)S(6)} %select_n.258, ...), kind=kOutput, calls=%fused_computation.61 | convolution fusion | flops 672382976 | bytes 10683908 | tf_op jit(solution)/shard_map/rcup,pv->rcuv/dot_general | solution.py:139
  75.2 4.6 subtract_reduce_fusion
  79.8 1.1 pad_maximum_fusion
  80.9 7.7 %gather_fusion.6 = bf16[128,2,64,256]{3,2,1,0:T(8,128)(2,1)} fusion(bf16[16,2,64,256]{3,2,0,1:T(8,128)(2,1)} %pad_maximum_fusion, s32[1024]{0:T(1024)S(1)} %pad_clamp_fusion.1), kind=kCustom, calls=%fused_computation.6 | custom fusion | bytes 16777728 | tf_op jit(solution)/shard_map/gather | solution.py:146
  88.6 6.0 %all-to-all-start.3 = ((bf16[16,8,2,64,256]{4,3,2,1,0:T(8,128)(2,1)}), bf16[16,8,2,64,256]{4,3,2,1,0:T(8,128)(2,1)}, u32[]{:S(2)}, u32[]{:S(2)}) async-start(bf16[16,8,2,64,256]{4,3,2,1,0:T(8,128)(2,1)} %bitcast.256), calls=%async_computation.3 | async-start | bytes 16777216 | tf_op jit(solution)/shard_map/all_to_all | solution.py:145
  94.7 20.8 %gather_fusion.2 = bf16[512,2,32,128]{3,2,1,0:T(8,128)(2,1)} fusion(bf16[64,2,32,128]{3,2,1,0:T(8,128)(2,1)} %param.9, s32[1024]{0:T(1024)S(1)} %pad_clamp_fusion.5), kind=kCustom, calls=%fused_computation.2 | custom fusion | bytes 16779264 | tf_op jit(solution)/shard_map/gather | solution.py:122
  115.5 161.7 %all-to-all-done.3 = bf16[16,8,2,64,256]{4,3,2,1,0:T(8,128)(2,1)} async-done(((bf16[16,8,2,64,256]{4,3,2,1,0:T(8,128)(2,1)}), bf16[16,8,2,64,256]{4,3,2,1,0:T(8,128)(2,1)}, u32[]{:S(2)}, u32[]{:S(2)}) %all-to-all-start.3) | async-done | bytes 8388640 | tf_op jit(solution)/shard_map/all_to_all | solution.py:145
  277.2 4.8 all-to-all-start.1
  282.5 6.5 %gather_fusion.4 = bf16[128,2,64,256]{3,2,1,0:T(8,128)(2,1)} fusion(bf16[40,2,64,256]{3,2,1,0:T(8,128)(2,1)S(1)} %copy-done, s32[1024]{0:T(1024)S(1)} %pad_clamp_fusion.3), kind=kCustom, calls=%fused_computation.4 | custom fusion | bytes 16777728 | tf_op jit(solution)/shard_map/gather | solution.py:83
  289.0 9.9 %gather_fusion.7 = bf16[128,2,64,256]{3,2,1,0:T(8,128)(2,1)} fusion(bf16[128,2,64,256]{3,2,1,0:T(8,128)(2,1)} %bitcast.36, s32[1024]{0:T(1024)S(1)} %pad_clamp_fusion), kind=kCustom, calls=%fused_computation.7 | custom fusion | bytes 16777728 | tf_op jit(solution)/shard_map/gather | solution.py:82
  298.9 8.5 %fusion.12 = (bf16[16,64,256]{2,1,0:T(8,128)(2,1)S(1)}, bf16[16,64,256]{2,1,0:T(8,128)(2,1)S(1)}) fusion(f32[16,8]{1,0:T(8,128)S(1)} %copy.125, bf16[16,8,2,64,256]{4,3,2,1,0:T(8,128)(2,1)} %bitcast.257, bf16[16,8,2,64,256]{4,3,2,1,0:T(8,128)(2,1)} %bitcast.253), kind=kLoop, calls=%fused_computation.34 | loop fusion | flops 28835840 | bytes 17826304 | tf_op jit(solution)/shard_map/reduce_sum | solution.py:89
  307.4 1.1 pad_maximum_fusion.1
  308.8 13.7 %gather_fusion = bf16[512,2,32,128]{3,2,1,0:T(8,128)(2,1)} fusion(bf16[40,2,32,128]{3,2,1,0:T(8,128)(2,1)S(1)} %copy-done.2, s32[1024]{0:T(1024)S(1)} %pad_clamp_fusion.7), kind=kCustom, calls=%fused_computation | custom fusion | bytes 16779264 | tf_op jit(solution)/shard_map/gather | solution.py:83
  322.5 1.9 multiply_cosine_fusion
  324.4 140.1 %all-to-all-done.1 = bf16[16,32,2,32,128]{4,3,2,1,0:T(8,128)(2,1)} async-done(((bf16[16,32,2,32,128]{4,3,2,1,0:T(8,128)(2,1)}), bf16[16,32,2,32,128]{4,3,2,1,0:T(8,128)(2,1)}, u32[]{:S(2)}, u32[]{:S(2)}) %all-to-all-start.1) | async-done | bytes 8388640 | tf_op jit(solution)/shard_map/all_to_all | solution.py:121
  464.6 22.9 %gather_fusion.3 = bf16[512,2,32,128]{3,2,1,0:T(8,128)(2,1)} fusion(bf16[512,2,32,128]{3,2,1,0:T(8,128)(2,1)} %bitcast.9, s32[1024]{0:T(1024)S(1)} %pad_clamp_fusion.4), kind=kCustom, calls=%fused_computation.3 | custom fusion | bytes 16779264 | tf_op jit(solution)/shard_map/gather | solution.py:82
  487.5 9.6 %fusion.3 = (f32[64,32,128]{2,1,0:T(8,128)}, f32[64,32,128]{2,1,0:T(8,128)}) fusion(f32[64,8]{1,0:T(8,128)S(1)} %copy.113, bf16[64,8,2,32,128]{4,3,2,1,0:T(8,128)(2,1)} %bitcast.255, bf16[64,8,2,32,128]{4,3,2,1,0:T(8,128)(2,1)} %bitcast.259), kind=kLoop, calls=%fused_computation.25 | loop fusion | flops 28835840 | bytes 18876416 | tf_op jit(solution)/shard_map/reduce_sum | solution.py:89
  497.0 1.9 fusion.40
  498.9 4.9 add_convert_fusion
  503.8 8.5 %fusion.34 = bf16[16,4,2,128,32]{3,4,2,1,0:T(8,128)(2,1)} fusion(bf16[16,4,1,128,256]{4,3,2,1,0:T(8,128)(2,1)} %get-tuple-element.22, bf16[16,4,1,128,256]{4,3,2,1,0:T(8,128)(2,1)} %get-tuple-element.21, f32[256,128]{1,0:T(8,128)S(1)} %cosine_reduce_fusion, f32[128]{0:T(128)S(1)} %get-tuple-element.37, f32[256]{0:T(256)S(1)} %iota_multiply_fusion, ...), kind=kOutput, calls=%fused_computation.65 | convolution fusion | flops 1215025152 | bytes 9587204 | tf_op jit(solution)/shard_map/tu,qkcup->qkctp/dot_general | solution.py:160
  512.3 3.2 fusion.28
  (83 shorter events, 7.5 us)
Async XLA Ops:
  6.5 275.9 %copy-start = (bf16[40,2,64,256]{3,2,1,0:T(8,128)(2,1)S(1)}, bf16[40,2,64,256]{3,2,1,0:T(8,128)(2,1)}, u32[]{:S(2)}) copy-start(bf16[40,2,64,256]{3,2,1,0:T(8,128)(2,1)} %param.17) | copy-start | bytes 7864324
  6.5 61.5 %all-gather.3.cloned.1.call-start = ((), (), s32[]{:S(2)}) async-start(), calls=%async_computation.4 | async-start | bytes 3145728 | tf_op jit(solution)/shard_map/all_gather | solution.py:136
  12.9 48.9 %all-to-all-start.2 = ((s32[16,1,8]{2,1,0:T(1,128)}), s32[16,1,8]{2,1,0:T(1,128)S(1)}, u32[]{:S(2)}, u32[]{:S(2)}) async-start(s32[16,1,8]{2,1,0:T(1,128)} %bitcast.33), calls=%async_computation.2 | async-start | bytes 16384 | tf_op jit(solution)/shard_map/all_to_all | solution.py:119
  61.7 26.8 %all-to-all-start = ((s32[16,1,32]{2,1,0:T(1,128)}), s32[16,1,32]{2,1,0:T(1,128)S(1)}, u32[]{:S(2)}, u32[]{:S(2)}) async-start(s32[16,1,32]{2,1,0:T(1,128)} %all_to_all.22), calls=%async_computation | async-start | bytes 16384 | tf_op jit(solution)/shard_map/all_to_all | solution.py:118
  88.6 188.6 %all-to-all-start.3 = ((bf16[16,8,2,64,256]{4,3,2,1,0:T(8,128)(2,1)}), bf16[16,8,2,64,256]{4,3,2,1,0:T(8,128)(2,1)}, u32[]{:S(2)}, u32[]{:S(2)}) async-start(bf16[16,8,2,64,256]{4,3,2,1,0:T(8,128)(2,1)} %bitcast.256), calls=%async_computation.3 | async-start | bytes 16777216 | tf_op jit(solution)/shard_map/all_to_all | solution.py:145
  277.2 5.1 copy-start.3
  277.2 187.4 %all-to-all-start.1 = ((bf16[16,32,2,32,128]{4,3,2,1,0:T(8,128)(2,1)}), bf16[16,32,2,32,128]{4,3,2,1,0:T(8,128)(2,1)}, u32[]{:S(2)}, u32[]{:S(2)}) async-start(bf16[16,32,2,32,128]{4,3,2,1,0:T(8,128)(2,1)} %bitcast.254), calls=%async_computation.1 | async-start | bytes 16777216 | tf_op jit(solution)/shard_map/all_to_all | solution.py:121
  282.0 215.0 %all-gather.5.cloned.1.call-start = ((), (), s32[]{:S(2)}) async-start(), calls=%async_computation.5 | async-start | bytes 3145728 | tf_op jit(solution)/shard_map/all_gather | solution.py:152
  298.9 9.7 %copy-start.4 = (s32[64,8]{0,1:T(8,128)S(1)}, s32[64,8]{0,1:T(8,128)}, u32[]{:S(2)}) copy-start(s32[64,8]{0,1:T(8,128)} %param.11) | copy-start | bytes 6148
  298.9 9.9 %copy-start.2 = (bf16[40,2,32,128]{3,2,1,0:T(8,128)(2,1)S(1)}, bf16[40,2,32,128]{3,2,1,0:T(8,128)(2,1)}, u32[]{:S(2)}) copy-start(bf16[40,2,32,128]{3,2,1,0:T(8,128)(2,1)} %param.13) | copy-start | bytes 1966084
  503.8 11.7 %copy-start.1 = (bf16[40,2,64,256]{3,2,1,0:T(8,128)(2,1)S(1)}, bf16[40,2,64,256]{3,2,1,0:T(8,128)(2,1)}, u32[]{:S(2)}) copy-start(bf16[40,2,64,256]{3,2,1,0:T(8,128)(2,1)} %param.17) | copy-start | bytes 7864324
Sparse Core Ops, SparseCore 0:
  8.9 33.2 all-gather.2
  308.6 33.0 all-gather.4
where the time goes:
time: 532 us; the launch traced here: 523 us
  waiting for transfers between devices  303 us (57%)
  local copies, waits for them, and re-layouts  95 us (18%)
  other arithmetic  72.1 us (14%)
  starting transfers between devices  23.3 us (4%)
  matrix products  15.7 us (3%)
  between operations  14.1 us (3%)
    all_to_all x1, waiting for transfers between devices, local(): lax.all_to_all(parent_field[parent_asked], 'box', split_axis=0, concat_ax...  162 us
    all_to_all x1, waiting for transfers between devices, local(): lax.all_to_all(child_field[child_asked], 'box', split_axis=0, concat_axis...  140 us
    gather x2, local copies, waits for them, and re-layouts, translate_sum(): source = flat_in[clipped].reshape((rows_here, slot_count) + pattern_shape)  32.8 us
    reduce_sum x2, other arithmetic, fourier_table(): jnp.sum(cosines, axis=2)  30.8 us
    gather x1, local copies, waits for them, and re-layouts, local(): child_field[child_asked]  20.8 us
    gather x2, local copies, waits for them, and re-layouts, translate_sum(): translator = op_table[op_index]  20.2 us
    reduce_sum x2, other arithmetic, translate_sum(): jnp.sum(weight * (op_real * src_real - op_imag * src_imag), axis=1)  18 us
  transfers between devices with their start and end apart: 6, of which 2 were waited for; matrix products, arithmetic and copies ran while one was open for 31% of the time, Pallas kernels for 0%

commit v1 on v0

v1 whole, which is shorter than its diff:
```python
import functools
import math

import jax
import jax.numpy as jnp
from jax import lax
from jax.experimental import pallas as pl
from jax.experimental.pallas import tpu as pltpu
from jax.sharding import PartitionSpec as P

CT = 64
SUBBOX_HEADINGS = 128
PT = 128
PP = 256
KIDS = 4
WAVE_NUMBER = 6.0


def waves(count, offset, half):
    doubled = (2 * jnp.arange(count, dtype=jnp.int32) + int(2 * offset))[:, None]
    harmonic = jnp.arange(half + 1, dtype=jnp.int32)[None, :]
    turns = (doubled * harmonic) % (2 * count)
    angle = turns.astype(jnp.float32) * (math.pi / count)
    return jnp.cos(angle), jnp.sin(angle)


def fourier_table(fine_count, coarse_count, offset):
    half = coarse_count // 2
    fine_cos, fine_sin = waves(fine_count, offset, half)
    coarse_cos, coarse_sin = waves(coarse_count, offset, half)
    order = jnp.arange(half + 1)
    weight = jnp.where((order == 0) | (order == half), 1.0, 2.0) / coarse_count
    fine = jnp.concatenate([fine_cos * weight, fine_sin * weight], axis=1)
    coarse = jnp.concatenate([coarse_cos, coarse_sin], axis=1)
    return jnp.dot(fine, coarse.T, precision=lax.Precision.HIGHEST)


def shift_parts(polar_rows):
    polar_angle = math.pi * (polar_rows.astype(jnp.float32) + 0.5) / PT
    heading_radians = 2.0 * math.pi / PP * jnp.arange(PP, dtype=jnp.float32)
    kid_index = jnp.arange(KIDS, dtype=jnp.int32)
    side_x = (2 * (kid_index % 2) - 1).astype(jnp.float32)
    side_y = (2 * (kid_index // 2 % 2) - 1).astype(jnp.float32)
    across = (
        side_x[:, None] * jnp.cos(heading_radians)[None, :]
        + side_y[:, None] * jnp.sin(heading_radians)[None, :]
    )
    phase_arg = WAVE_NUMBER * jnp.sin(polar_angle)[None, :, None] * across[:, None, :]
    return (jnp.cos(phase_arg), jnp.sin(phase_arg))


def lift_sum(widened, cos_part, sin_part):
    real_part = jnp.sum(
        cos_part * widened[..., 0, :, :] - sin_part * widened[..., 1, :, :], axis=-3
    )
    imag_part = jnp.sum(
        cos_part * widened[..., 1, :, :] + sin_part * widened[..., 0, :, :], axis=-3
    )
    return jnp.stack([real_part, imag_part], axis=-3).astype(jnp.bfloat16)


def lower_turn(parents, cos_part, sin_part):
    real_in = jnp.expand_dims(parents[..., 0, :, :].astype(jnp.float32), -3)
    imag_in = jnp.expand_dims(parents[..., 1, :, :].astype(jnp.float32), -3)
    real_out = cos_part * real_in + sin_part * imag_in
    imag_out = cos_part * imag_in - sin_part * real_in
    return jnp.stack([real_out, imag_out], axis=-3).astype(jnp.bfloat16)


def far_kernel(span, list_ref, op_ref, home_ref, field_ref, ops_ref, out_ref, padded):
    rows, slots = list_ref.shape
    empty = ops_ref.shape[0]
    padded[0:empty] = ops_ref[...]
    padded[empty] = jnp.zeros_like(padded[empty])
    thin = out_ref.shape[2]

    def row(r, carry):
        homes, opers = [], []
        for j in range(slots):
            box = list_ref[r, j]
            homes.append(home_ref[jnp.maximum(box, 0)])
            opers.append(jnp.where(box >= 0, op_ref[r, j], empty))
        for start in range(0, thin, span):
            part = pl.ds(start, span)
            real = imag = None
            for j in range(slots):
                a = padded[opers[j], 0, part, :].astype(jnp.float32)
                b = padded[opers[j], 1, part, :].astype(jnp.float32)
                c = field_ref[homes[j], 0, part, :].astype(jnp.float32)
                d = field_ref[homes[j], 1, part, :].astype(jnp.float32)
                re, im = a * c - b * d, a * d + b * c
                real = re if real is None else real + re
                imag = im if imag is None else imag + im
            out_ref[r, 0, part, :] = real.astype(out_ref.dtype)
            out_ref[r, 1, part, :] = imag.astype(out_ref.dtype)
        return carry

    lax.fori_loop(0, rows, row, 0)


def far_sum(field, lists, ops, homes, table, dtype):
    rows, slots = lists.shape
    shape = field.shape[1:]
    span = min(shape[1], 4096 // shape[2])
    smem = pl.BlockSpec(memory_space=pltpu.SMEM)
    vmem = pl.BlockSpec(memory_space=pltpu.VMEM)
    return pl.pallas_call(
        functools.partial(far_kernel, span),
        out_shape=jax.ShapeDtypeStruct((rows,) + shape, dtype),
        in_specs=[smem, smem, smem, vmem, vmem],
        out_specs=vmem,
        scratch_shapes=[pltpu.VMEM((table.shape[0] + 1,) + table.shape[1:], table.dtype)],
        compiler_params=pltpu.CompilerParams(vmem_limit_bytes=32 * 2**20),
        cost_estimate=pl.CostEstimate(
            flops=rows * slots * math.prod(shape) * 4,
            bytes_accessed=field.size * 2 + table.size * 2,
            transcendentals=0,
        ),
    )(lists, ops, homes, field, table)


def local(
    child_field,
    child_list,
    child_op,
    child_home,
    child_ops,
    parent_list,
    parent_op,
    parent_home,
    parent_ops,
):
    angle_index = lax.axis_index("angle")
    child_rows = child_field.shape[0]
    parent_rows = parent_list.shape[0]
    child_thin = child_field.shape[2]
    parent_thin = parent_ops.shape[2]
    whole_polar = lax.all_gather(child_field, "angle", axis=2, tiled=True)
    child_all = lax.all_gather(child_field, "box", axis=0, tiled=True)
    theta = fourier_table(PT, CT, 0.5)
    phi = fourier_table(PP, SUBBOX_HEADINGS, 0.0)
    theta_up = theta.astype(jnp.bfloat16)
    phi_up = phi.T.astype(jnp.bfloat16)
    theta_down = (theta.T * (CT / PT)).astype(jnp.bfloat16)
    phi_down = (phi * (SUBBOX_HEADINGS / PP)).astype(jnp.bfloat16)
    up_rows = lax.dynamic_slice_in_dim(theta_up, angle_index * parent_thin, parent_thin, 0)
    stretched = jnp.einsum(
        "ut,rctp->rcup", up_rows, whole_polar, preferred_element_type=jnp.float32
    ).astype(jnp.bfloat16)
    widened = jnp.einsum("rcup,pv->rcuv", stretched, phi_up, preferred_element_type=jnp.float32)
    local_polar = angle_index * parent_thin + jnp.arange(parent_thin, dtype=jnp.int32)
    cos_local, sin_local = shift_parts(local_polar)
    parent_field = lift_sum(
        widened.reshape(parent_rows, KIDS, 2, parent_thin, PP), cos_local, sin_local
    )
    parent_all = lax.all_gather(parent_field, "box", axis=0, tiled=True)
    child_far = far_sum(child_all, child_list, child_op, child_home, child_ops, jnp.float32)
    parent_far = far_sum(
        parent_all, parent_list, parent_op, parent_home, parent_ops, jnp.bfloat16
    )
    down_rows = lax.dynamic_slice_in_dim(theta_down, angle_index * child_thin, child_thin, 0)
    parents = lax.all_gather(parent_far, "angle", axis=2, tiled=True)
    cos_piece, sin_piece = shift_parts(jnp.arange(PT, dtype=jnp.int32))
    turned = lower_turn(parents, cos_piece, sin_piece)
    narrowed = jnp.einsum(
        "qkcuv,vp->qkcup", turned, phi_down, preferred_element_type=jnp.float32
    ).astype(jnp.bfloat16)
    summed_term = jnp.einsum(
        "tu,qkcup->qkctp", down_rows, narrowed, preferred_element_type=jnp.float32
    )
    child_term = summed_term.astype(jnp.bfloat16).reshape(
        child_rows, 2, child_thin, SUBBOX_HEADINGS
    )
    child_term = lax.optimization_barrier(child_term)
    return (child_far + child_term.astype(jnp.float32)).astype(jnp.bfloat16)


def solution(mesh):
    return jax.shard_map(
        local,
        mesh=mesh,
        in_specs=(
            P("box", None, "angle", None),
            P("box", None),
            P("box", None),
            P(),
            P(None, None, "angle", None),
            P("box", None),
            P("box", None),
            P(),
            P(None, None, "angle", None),
        ),
        out_specs=P("box", None, "angle", None),
        check_vma=False,
    )
```

time: 532 us -> 366 us (0.69)
  the two profiles are of different devices: /device:TPU:18 before, /device:TPU:0 now
where the time goes in v1:
time: 366 us
  waiting for transfers between devices  294 us (80%)
  other arithmetic  19.1 us (5%)
  matrix products  14.4 us (4%)
  between operations  13.3 us (4%)
  Pallas kernels  12.9 us (4%)
  local copies, waits for them, and re-layouts  12 us (3%)
    all_gather x1, waiting for transfers between devices, local(): parent_all = lax.all_gather(parent_field, 'box', axis=0, tiled=True)  126 us
    all_gather x1, waiting for transfers between devices, local(): child_all = lax.all_gather(child_field, 'box', axis=0, tiled=True)  112 us
    all_gather x1, waiting for transfers between devices, local(): whole_polar = lax.all_gather(child_field, 'angle', axis=2, tiled=True)  34.2 us
    all_gather x1, waiting for transfers between devices, local(): parents = lax.all_gather(parent_far, 'angle', axis=2, tiled=True)  19.9 us
    pallas_call x2, Pallas kernels, far_sum(): pl.pallas_call(functools.partial(far_kernel, span), out_shape=jax.ShapeDt...  12.9 us
    unnamed x28, local copies, waits for them, and re-layouts  12 us
  transfers between devices with their start and end apart: 4, of which 4 were waited for; matrix products, arithmetic and copies ran while one was open for 2% of the time, Pallas kernels for 4%

profile of v1, /device:TPU:0, one launch (start us, length us, event | category | flops | bytes accessed | tf_op | source)
XLA Modules:
  0.0 365.9 jit_solution(6522093560077008701)
XLA Ops:
  6.5 0.7 all-gather.7.cloned.1.call-update
  7.5 0.1 cosine_multiply_fusion.1
  7.6 0.2 fusion.74
  7.8 0.2 fusion.48
  8.0 0.3 fusion.59
  8.4 0.6 cosine_multiply_fusion
  9.0 0.4 fusion.22
  9.4 0.1 multiply_add_fusion
  9.5 1.0 multiply_cosine_fusion.1
  10.5 34.2 %all-gather.7.cloned.1.call-done = bf16[64,2,64,128]{3,2,1,0:T(8,128)(2,1)} async-done(((bf16[64,2,32,128]{3,2,1,0:T(8,128)(2,1)}), bf16[64,2,64,128]{3,2,1,0:T(8,128)(2,1)}) %all-gather.7.cloned.1.call-update) | async-done | bytes 2097168 | tf_op jit(solution)/shard_map/all_gather | solution.py:138
  44.7 6.8 %fusion.10 = f32[64,2,64,256]{3,2,1,0:T(8,128)} fusion(bf16[64,2,64,128]{3,2,1,0:T(8,128)(2,1)} %all-gather.7.cloned.1.call-done, f32[256,128]{1,0:T(8,128)S(1)} %fusion.22, f32[128,64]{0,1:T(8,128)S(1)} %fusion.48, s32[]{:T(128)S(6)} %select_n.121), kind=kOutput, calls=%fused_computation.12 | convolution fusion | flops 672169984 | bytes 10633220 | tf_op jit(solution)/shard_map/rcup,pv->rcuv/dot_general | solution.py:150
  51.5 4.6 %subtract_reduce_fusion = (bf16[16,64,256]{2,1,0:T(8,128)(2,1)S(1)}, bf16[16,64,256]{2,1,0:T(8,128)(2,1)S(1)}) fusion(f32[16,4,2,64,256]{4,3,2,1,0:T(8,128)} %bitcast.58, f32[4,64,256]{2,1,0:T(8,128)S(1)} %get-tuple-element.14, f32[4,64,256]{2,1,0:T(8,128)S(1)} %get-tuple-element.13), kind=kLoop, calls=%fused_computation.11 | loop fusion | flops 7864320 | bytes 9961472 | tf_op jit(solution)/shard_map/reduce_sum | solution.py:53
  56.2 1.1 pad_maximum_fusion
  57.3 0.0 all-gather.5.cloned.1.call-start
  57.3 0.7 all-gather.5.cloned.1.call-update
  58.0 0.2 all-gather.11.cloned.1.call-start
  58.3 0.1 copy.24.list_ref
  58.3 0.1 copy.25.op_ref
  58.4 125.9 %all-gather.9.cloned.1.call-done.field_ref = bf16[256,2,64,256]{3,2,1,0:T(8,128)(2,1)} async-done(((bf16[16,2,64,256]{3,2,1,0:T(8,128)(2,1)}), bf16[256,2,64,256]{3,2,1,0:T(8,128)(2,1)}) %all-gather.9.cloned.1.call-update) | async-done | bytes 16777232 | tf_op jit(solution)/shard_map/all_gather | solution.py:156
  184.4 5.8 %copy-done.1 = bf16[256,2,64,256]{3,2,1,0:T(8,128)(2,1)S(1)} copy-done((bf16[256,2,64,256]{3,2,1,0:T(8,128)(2,1)S(1)}, bf16[256,2,64,256]{3,2,1,0:T(8,128)(2,1)}, u32[]{:S(2)}) %copy-start.1) | copy-done | bytes 16777240
  190.1 6.0 %shard_map.92 = bf16[16,2,64,256]{3,2,1,0:T(8,128)(2,1)} custom-call(s32[16,8]{1,0:T(8,128)S(1)} %copy.24.list_ref, s32[16,8]{1,0:T(8,128)S(1)} %copy.25.op_ref, s32[256]{0:T(256)S(1)} %copy-done.5, bf16[256,2,64,256]{3,2,1,0:T(8,128)(2,1)S(1)} %copy-done.1, bf16[40,2,64,256]{3,2,1,0:T(8,128)(2,1)S(1)} %copy-done.2), custom_call_target="tpu_custom_call" | custom-call | flops 16777216 | bytes 19398656 | tf_op jit(solution)/shard_map/pallas_call | solution.py:107
  196.2 0.1 copy.20.list_ref
  196.3 0.1 copy.21.op_ref
  196.4 2.8 multiply_cosine_fusion
  199.2 112.4 %all-gather.5.cloned.1.call-done.field_ref = bf16[1024,2,32,128]{3,2,1,0:T(8,128)(2,1)} async-done(((bf16[64,2,32,128]{3,2,1,0:T(8,128)(2,1)}), bf16[1024,2,32,128]{3,2,1,0:T(8,128)(2,1)}) %all-gather.5.cloned.1.call-update) | async-done | bytes 16777232 | tf_op jit(solution)/shard_map/all_gather | solution.py:139
  311.6 5.9 %copy-done = bf16[1024,2,32,128]{3,2,1,0:T(8,128)(2,1)S(1)} copy-done((bf16[1024,2,32,128]{3,2,1,0:T(8,128)(2,1)S(1)}, bf16[1024,2,32,128]{3,2,1,0:T(8,128)(2,1)}, u32[]{:S(2)}) %copy-start) | copy-done | bytes 16777240
  317.5 6.9 %shard_map.91 = f32[64,2,32,128]{3,2,1,0:T(8,128)S(1)} custom-call(s32[64,8]{1,0:T(8,128)S(1)} %copy.20.list_ref, s32[64,8]{1,0:T(8,128)S(1)} %copy.21.op_ref, s32[1024]{0:T(1024)S(1)} %copy-done.4, bf16[1024,2,32,128]{3,2,1,0:T(8,128)(2,1)S(1)} %copy-done, bf16[40,2,32,128]{3,2,1,0:T(8,128)(2,1)S(1)} %copy-done.3), custom_call_target="tpu_custom_call" | custom-call | flops 16777216 | bytes 17432576 | tf_op jit(solution)/shard_map/pallas_call | solution.py:107
  324.4 19.9 %all-gather.11.cloned.1.call-done = bf16[16,2,128,256]{3,2,1,0:T(8,128)(2,1)} async-done(((bf16[16,2,64,256]{3,2,1,0:T(8,128)(2,1)}), bf16[16,2,128,256]{3,2,1,0:T(8,128)(2,1)}) %all-gather.11.cloned.1.call-update) | async-done | bytes 2097168 | tf_op jit(solution)/shard_map/all_gather | solution.py:162
  344.3 2.0 fusion.21
  346.4 4.8 %add_convert_fusion = (bf16[16,4,1,128,256]{4,3,2,1,0:T(8,128)(2,1)}, bf16[16,4,1,128,256]{4,3,2,1,0:T(8,128)(2,1)}) fusion(f32[16,128,256]{2,1,0:T(8,128)S(1)} %get-tuple-element.10, f32[4,128,256]{2,1,0:T(8,128)S(1)} %copy-done.7, f32[16,128,256]{2,1,0:T(8,128)S(1)} %get-tuple-element.9, f32[4,128,256]{2,1,0:T(8,128)S(1)} %copy-done.6), kind=kLoop, calls=%fused_computation.5 | loop fusion | flops 16777216 | bytes 13631488 | tf_op jit(solution)/shard_map/convert.2
  351.2 6.9 %fusion.15 = bf16[16,4,2,128,32]{3,4,2,1,0:T(8,128)(2,1)S(1)} fusion(bf16[16,4,1,128,256]{4,3,2,1,0:T(8,128)(2,1)} %get-tuple-element.8, bf16[16,4,1,128,256]{4,3,2,1,0:T(8,128)(2,1)} %get-tuple-element.7, f32[256,128]{1,0:T(8,128)S(1)} %fusion.22, f32[128,64]{0,1:T(8,128)S(1)} %fusion.48, s32[]{:T(128)S(6)} %select_n.125), kind=kOutput, calls=%fused_computation.17 | convolution fusion | flops 1214849024 | bytes 9584644 | tf_op jit(solution)/shard_map/tu,qkcup->qkctp/dot_general | solution.py:168
  358.1 1.3 add_convert_fusion.1
  (36 shorter events, 0.3 us)
Async XLA Ops:
  6.5 38.2 %all-gather.7.cloned.1.call-start = ((), (), s32[]{:S(2)}) async-start(), calls=%async_computation.1 | async-start | bytes 3145728 | tf_op jit(solution)/shard_map/all_gather | solution.py:138
  7.3 177.1 %all-gather.9.cloned.1.call-start = ((), (), s32[]{:S(2)}) async-start(), calls=%async_computation.2 | async-start | bytes 17825792 | tf_op jit(solution)/shard_map/all_gather | solution.py:156
  56.1 2.1 copy-start.8
  56.2 2.2 copy-start.9
  56.2 128.2 %copy-start.2 = (bf16[40,2,64,256]{3,2,1,0:T(8,128)(2,1)S(1)}, bf16[40,2,64,256]{3,2,1,0:T(8,128)(2,1)}, u32[]{:S(2)}) copy-start(bf16[40,2,64,256]{3,2,1,0:T(8,128)(2,1)} %ops_ref.3) | copy-start | bytes 7864324
  56.2 128.2 %copy-start.5 = (s32[256]{0:T(256)S(1)}, s32[256]{0:T(256)}, u32[]{:S(2)}) copy-start(s32[256]{0:T(256)} %home_ref.3) | copy-start | bytes 3076
  57.3 254.3 %all-gather.5.cloned.1.call-start = ((), (), s32[]{:S(2)}) async-start(), calls=%async_computation | async-start | bytes 17825792 | tf_op jit(solution)/shard_map/all_gather | solution.py:139
  58.0 286.3 %all-gather.11.cloned.1.call-start = ((), (), s32[]{:S(2)}) async-start(), calls=%async_computation.3 | async-start | bytes 3145728 | tf_op jit(solution)/shard_map/all_gather | solution.py:162
  184.4 5.8 %copy-start.1 = (bf16[256,2,64,256]{3,2,1,0:T(8,128)(2,1)S(1)}, bf16[256,2,64,256]{3,2,1,0:T(8,128)(2,1)}, u32[]{:S(2)}) copy-start(bf16[256,2,64,256]{3,2,1,0:T(8,128)(2,1)} %all-gather.9.cloned.1.call-done.field_ref) | copy-start | bytes 50331652
  190.1 6.0 %copy-start.10 = (s32[64,8]{0,1:T(8,128)S(1)}, s32[64,8]{0,1:T(8,128)}, u32[]{:S(2)}) copy-start(s32[64,8]{0,1:T(8,128)} %param.10) | copy-start | bytes 6148
  190.1 6.1 %copy-start.11 = (s32[64,8]{0,1:T(8,128)S(1)}, s32[64,8]{0,1:T(8,128)}, u32[]{:S(2)}) copy-start(s32[64,8]{0,1:T(8,128)} %param.11) | copy-start | bytes 6148
  190.1 121.5 %copy-start.3 = (bf16[40,2,32,128]{3,2,1,0:T(8,128)(2,1)S(1)}, bf16[40,2,32,128]{3,2,1,0:T(8,128)(2,1)}, u32[]{:S(2)}) copy-start(bf16[40,2,32,128]{3,2,1,0:T(8,128)(2,1)} %ops_ref.2) | copy-start | bytes 1966084
  190.1 121.5 %copy-start.4 = (s32[1024]{0:T(1024)S(1)}, s32[1024]{0:T(1024)}, u32[]{:S(2)}) copy-start(s32[1024]{0:T(1024)} %home_ref.2) | copy-start | bytes 12292
  311.6 5.9 %copy-start = (bf16[1024,2,32,128]{3,2,1,0:T(8,128)(2,1)S(1)}, bf16[1024,2,32,128]{3,2,1,0:T(8,128)(2,1)}, u32[]{:S(2)}) copy-start(bf16[1024,2,32,128]{3,2,1,0:T(8,128)(2,1)} %all-gather.5.cloned.1.call-done.field_ref) | copy-start | bytes 50331652
  324.4 22.0 %copy-start.6 = (f32[4,128,256]{2,1,0:T(8,128)S(1)}, f32[4,128,256]{2,1,0:T(8,128)}, u32[]{:S(2)}) copy-start(f32[4,128,256]{2,1,0:T(8,128)} %get-tuple-element.11) | copy-start | bytes 1572868
  324.4 22.0 %copy-start.7 = (f32[4,128,256]{2,1,0:T(8,128)S(1)}, f32[4,128,256]{2,1,0:T(8,128)}, u32[]{:S(2)}) copy-start(f32[4,128,256]{2,1,0:T(8,128)} %get-tuple-element.12) | copy-start | bytes 1572868
Sparse Core Ops, SparseCore 0:
  8.9 35.8 all-gather.6
  57.4 126.8 all-gather.8
  186.5 125.0 all-gather.4
  313.0 31.2 all-gather.10

commit v2 on v1

--- a/solution.py
+++ b/solution.py
@@ -119,6 +119,330 @@
     )(lists, ops, homes, field, table)
 
 
+Z, Y, C = 4, 2, 2
+UP, DOWN, SIDE, CORE, PAIR = range(5)
+CHUNKS = 4
+
+
+class Gather:
+    def __init__(self, own, slots, rows, send, recv, place):
+        self.own, self.slots, self.rows, self.send, self.recv = own, slots, rows, send, recv
+        self.z, self.y, self.c = place
+        self.started = []
+
+    def slot(self, z, y, c):
+        return (z * Y + y) * C + c
+
+    def part(self, slot, h):
+        half = self.rows // 2
+        return self.slots.at[pl.ds(slot * self.rows + h * half, half)]
+
+    def copy(self, slot, h, way, target, first=False):
+        half = self.rows // 2
+        source = self.own.at[pl.ds(h * half, half)] if first else self.part(slot, h)
+        return pltpu.make_async_remote_copy(
+            src_ref=source,
+            dst_ref=self.part(slot, h),
+            send_sem=self.send.at[way, slot, h],
+            recv_sem=self.recv.at[slot, h],
+            device_id={"box": target},
+            device_id_type=pl.DeviceIdType.MESH,
+        )
+
+    def go(self, cond, *args, **kw):
+        copy = self.copy(*args, **kw)
+        self.started.append((cond, copy))
+        pl.when(cond)(lambda: copy.start()) if cond is not None else copy.start()
+
+    def near(self, way):
+        z, y, c = self.z, self.y, self.c
+        if way == UP:
+            return self.slot(jnp.minimum(z + 1, Z - 1), y, c)
+        if way == DOWN:
+            return self.slot(jnp.maximum(z - 1, 0), y, c)
+        if way == SIDE:
+            return self.slot(z, 1 - y, c)
+        if way == CORE:
+            return self.slot(z, y, 1 - c)
+        return self.slot(z + 1 - 2 * (z % 2), y, c)
+
+    def arrived(self, cond, slot, h):
+        copy = self.copy(slot, h, CORE, self.near(CORE))
+        pl.when(cond)(lambda: copy.wait_recv()) if cond is not None else copy.wait_recv()
+
+    def first(self, h):
+        mine = self.slot(self.z, self.y, self.c)
+        self.go(self.z < Z - 1, mine, h, UP, self.near(UP), first=True)
+        self.go(self.z > 0, mine, h, DOWN, self.near(DOWN), first=True)
+        self.go(None, mine, h, SIDE, self.near(SIDE), first=True)
+        self.go(None, mine, h, CORE, self.near(CORE), first=True)
+
+    def across(self, d):
+        for sign in (-1, 1) if d else (1,):
+            there = self.z + sign * d
+            valid = None if d == 0 else (there >= 0) & (there < Z)
+            slot = self.slot(jnp.clip(there, 0, Z - 1), 1 - self.y, self.c)
+            for h in range(2):
+                self.arrived(valid, slot, h)
+                self.go(valid, slot, h, CORE, self.near(CORE))
+                if d == 0 and h == 1:
+                    self.go(None, slot, h, PAIR, self.near(PAIR))
+
+    def step(self, d):
+        for h in range(2):
+            for sign in (-1, 1):
+                there = self.z + sign * d
+                valid = (there >= 0) & (there < Z)
+                slot = self.slot(jnp.clip(there, 0, Z - 1), self.y, self.c)
+                self.arrived(valid, slot, h)
+                onward = valid & ((self.z < Z - 1) if sign < 0 else (self.z > 0))
+                self.go(onward, slot, h, UP if sign < 0 else DOWN, self.near(UP if sign < 0 else DOWN))
+                side = valid
+                if d == 1 and h == 1:
+                    side = valid & ((self.z % 2 == 1) if sign < 0 else (self.z % 2 == 0))
+                    side = valid & jnp.logical_not(side)
+                self.go(side, slot, h, SIDE, self.near(SIDE))
+                self.go(valid, slot, h, CORE, self.near(CORE))
+        self.across(d - 1)
+
+    def finish(self):
+        self.across(Z - 1)
+        for z in range(Z):
+            for y in range(Y):
+                for h in range(2):
+                    self.arrived(None, self.slot(z, y, 1 - self.c), h)
+
+    def drain(self):
+        for cond, copy in self.started:
+            pl.when(cond)(lambda copy=copy: copy.wait_send()) if cond is not None else copy.wait_send()
+
+
+def translate(lists, op, home, field, padded, r, empty, start, span):
+    part = pl.ds(start, span)
+    real = imag = None
+    for j in range(lists.shape[1]):
+        box = lists[r, j]
+        at = home[jnp.maximum(box, 0)]
+        oper = jnp.where(box >= 0, op[r, j], empty)
+        a = padded[oper, 0, part, :].astype(jnp.float32)
+        b = padded[oper, 1, part, :].astype(jnp.float32)
+        c = field[at, 0, part, :].astype(jnp.float32)
+        d = field[at, 1, part, :].astype(jnp.float32)
+        re, im = a * c - b * d, a * d + b * c
+        real = re if real is None else real + re
+        imag = im if imag is None else imag + im
+    return real, imag
+
+
+def whole_kernel(
+    child_field, child_list, child_op, child_home, child_ops,
+    parent_list, parent_op, parent_home, parent_ops,
+    theta_up, phi_up, theta_down, phi_down, cos_ref, sin_ref,
+    out_ref,
+    child_all, parent_all, polar, child_pad, parent_pad, far, terms,
+    c_send, c_recv, p_send, p_recv, x_send, x_recv, f_send, f_recv, here,
+):
+    box, angle = lax.axis_index("box"), lax.axis_index("angle")
+    z, y, c = box // (Y * C), (box // C) % Y, box % C
+    children, child_thin = child_field.shape[0], child_field.shape[2]
+    parents, parent_thin = parent_list.shape[0], far.shape[3]
+    kids_rows, group = children // CHUNKS, parents // CHUNKS
+    child_empty, parent_empty = child_ops.shape[0], parent_ops.shape[0]
+    MESH = pl.DeviceIdType.MESH
+    children_of = Gather(child_field, child_all, children, c_send, c_recv, (z, y, c))
+    mine = parent_all.at[pl.ds(box * parents, parents)]
+    parents_of = Gather(mine, parent_all, parents, p_send, p_recv, (z, y, c))
+    other = {"angle": 1 - angle}
+
+    locals_ = [
+        pltpu.make_async_copy(child_field, polar.at[angle], here.at[0]),
+        pltpu.make_async_copy(child_field, child_all.at[pl.ds(box * children, children)], here.at[1]),
+        pltpu.make_async_copy(child_ops, child_pad.at[pl.ds(0, child_empty)], here.at[2]),
+        pltpu.make_async_copy(parent_ops, parent_pad.at[pl.ds(0, parent_empty)], here.at[3]),
+    ]
+    for copy in locals_:
+        copy.start()
+
+    barrier = pltpu.get_barrier_semaphore()
+    for way in (SIDE, CORE):
+        pl.semaphore_signal(barrier, inc=1, device_id={"box": children_of.near(way)}, device_id_type=MESH)
+    pl.semaphore_signal(barrier, inc=1, device_id=other, device_id_type=MESH)
+
+    @pl.when(z < Z - 1)
+    def _():
+        pl.semaphore_signal(barrier, inc=1, device_id={"box": children_of.near(UP)}, device_id_type=MESH)
+
+    @pl.when(z > 0)
+    def _():
+        pl.semaphore_signal(barrier, inc=1, device_id={"box": children_of.near(DOWN)}, device_id_type=MESH)
+
+    pl.semaphore_wait(barrier, 5 - (z == 0).astype(jnp.int32) - (z == Z - 1).astype(jnp.int32))
+
+    crossing = []
+    for i in range(CHUNKS):
+        rows = pl.ds(i * kids_rows, kids_rows)
+        crossing.append(
+            pltpu.make_async_remote_copy(
+                src_ref=child_field.at[rows], dst_ref=polar.at[angle, rows],
+                send_sem=x_send.at[i], recv_sem=x_recv.at[i],
+                device_id=other, device_id_type=MESH,
+            )
+        )
+        crossing[-1].start()
+    for h in range(2):
+        children_of.first(h)
+    child_pad[child_empty] = jnp.zeros(child_pad.shape[1:], child_pad.dtype)
+    parent_pad[parent_empty] = jnp.zeros(parent_pad.shape[1:], parent_pad.dtype)
+    for copy in locals_:
+        copy.wait()
+
+    up = theta_up[pl.ds(pl.multiple_of(angle * parent_thin, parent_thin), parent_thin), :]
+    here_rows = pl.ds(pl.multiple_of(angle * parent_thin, parent_thin), parent_thin)
+
+    def lift(q, carry):
+        columns = [
+            jnp.concatenate([polar[0, q * KIDS + k, ri], polar[1, q * KIDS + k, ri]], axis=0)
+            for k in range(KIDS) for ri in range(2)
+        ]
+        stretched = jnp.dot(
+            up, jnp.concatenate(columns, axis=1), preferred_element_type=jnp.float32
+        ).astype(jnp.bfloat16)
+        stacked = jnp.concatenate(
+            [stretched[:, i * SUBBOX_HEADINGS : (i + 1) * SUBBOX_HEADINGS] for i in range(2 * KIDS)],
+            axis=0,
+        )
+        wide = jnp.dot(stacked, phi_up[...], preferred_element_type=jnp.float32)
+        real = imag = 0.0
+        for k in range(KIDS):
+            co, si = cos_ref[k, here_rows, :], sin_ref[k, here_rows, :]
+            wr = wide[2 * k * parent_thin : (2 * k + 1) * parent_thin]
+            wi = wide[(2 * k + 1) * parent_thin : (2 * k + 2) * parent_thin]
+            real = real + (co * wr - si * wi)
+            imag = imag + (co * wi + si * wr)
+        parent_all[box * parents + q, 0] = real.astype(jnp.bfloat16)
+        parent_all[box * parents + q, 1] = imag.astype(jnp.bfloat16)
+        return carry
+
+    for i in range(CHUNKS):
+        crossing[i].wait_recv()
+        lax.fori_loop(i * group, (i + 1) * group, lift, 0)
+        if i % 2:
+            parents_of.first(i // 2)
+
+    parents_of.step(1)
+    children_of.step(1)
+    parents_of.step(2)
+    parents_of.step(3)
+    parents_of.finish()
+    children_of.step(2)
+
+    span = min(parent_thin, 4096 // PP)
+
+    def parent_row(r, carry):
+        for start in range(0, parent_thin, span):
+            real, imag = translate(
+                parent_list, parent_op, parent_home, parent_all, parent_pad, r, parent_empty, start, span
+            )
+            far[angle, r, 0, pl.ds(start, span), :] = real.astype(jnp.bfloat16)
+            far[angle, r, 1, pl.ds(start, span), :] = imag.astype(jnp.bfloat16)
+        return carry
+
+    back = []
+    for i in range(CHUNKS):
+        lax.fori_loop(i * group, (i + 1) * group, parent_row, 0)
+        rows = far.at[angle, pl.ds(i * group, group)]
+        back.append(
+            pltpu.make_async_remote_copy(
+                src_ref=rows, dst_ref=rows, send_sem=f_send.at[i], recv_sem=f_recv.at[i],
+                device_id=other, device_id_type=MESH,
+            )
+        )
+        back[-1].start()
+
+    down = theta_down[pl.ds(pl.multiple_of(angle * child_thin, child_thin), child_thin), :]
+
+    def lower(q, carry):
+        turned = []
+        for k in range(KIDS):
+            reals, imags = [], []
+            for a in range(PT // parent_thin):
+                rows = pl.ds(a * parent_thin, parent_thin)
+                co, si = cos_ref[k, rows, :], sin_ref[k, rows, :]
+                real, imag = far[a, q, 0].astype(jnp.float32), far[a, q, 1].astype(jnp.float32)
+                reals.append((co * real + si * imag).astype(jnp.bfloat16))
+                imags.append((co * imag - si * real).astype(jnp.bfloat16))
+            turned += reals + imags
+        narrowed = jnp.dot(
+            jnp.concatenate(turned, axis=0), phi_down[...], preferred_element_type=jnp.float32
+        ).astype(jnp.bfloat16)
+        columns = jnp.concatenate([narrowed[i * PT : (i + 1) * PT] for i in range(2 * KIDS)], axis=1)
+        summed = jnp.dot(down, columns, preferred_element_type=jnp.float32).astype(jnp.bfloat16)
+        for k in range(KIDS):
+            for ri in range(2):
+                i = 2 * k + ri
+                terms[q * KIDS + k, ri] = summed[:, i * SUBBOX_HEADINGS : (i + 1) * SUBBOX_HEADINGS]
+        return carry
+
+    for i in range(CHUNKS):
+        back[i].wait_recv()
+        lax.fori_loop(i * group, (i + 1) * group, lower, 0)
+
+    children_of.step(3)
+    children_of.finish()
+
+    def child_row(r, carry):
+        real, imag = translate(
+            child_list, child_op, child_home, child_all, child_pad, r, child_empty, 0, child_thin
+        )
+        out_ref[r, 0] = (real + terms[r, 0].astype(jnp.float32)).astype(jnp.bfloat16)
+        out_ref[r, 1] = (imag + terms[r, 1].astype(jnp.float32)).astype(jnp.bfloat16)
+        return carry
+
+    lax.fori_loop(0, children, child_row, 0)
+    children_of.drain()
+    parents_of.drain()
+    for copy in crossing + back:
+        copy.wait_send()
+
+
+def whole(fields, tables):
+    child_field, child_list, _, _, child_ops, parent_list, _, _, parent_ops = fields
+    owners, angles = lax.axis_size("box"), lax.axis_size("angle")
+    parent_shape = (parent_list.shape[0], 2) + parent_ops.shape[2:]
+    smem = pl.BlockSpec(memory_space=pltpu.SMEM)
+    vmem = pl.BlockSpec(memory_space=pltpu.VMEM)
+    hbm = pl.BlockSpec(memory_space=pl.ANY)
+    bf16 = jnp.bfloat16
+    dma = pltpu.SemaphoreType.DMA
+    return pl.pallas_call(
+        whole_kernel,
+        out_shape=jax.ShapeDtypeStruct(child_field.shape, bf16),
+        in_specs=[hbm, smem, smem, smem, hbm, smem, smem, smem, hbm] + [vmem] * 6,
+        out_specs=vmem,
+        scratch_shapes=[
+            pltpu.VMEM((owners * child_field.shape[0],) + child_field.shape[1:], bf16),
+            pltpu.VMEM((owners * parent_shape[0],) + parent_shape[1:], bf16),
+            pltpu.VMEM((angles,) + child_field.shape, bf16),
+            pltpu.VMEM((child_ops.shape[0] + 1,) + child_ops.shape[1:], bf16),
+            pltpu.VMEM((parent_ops.shape[0] + 1,) + parent_ops.shape[1:], bf16),
+            pltpu.VMEM((angles,) + parent_shape, bf16),
+            pltpu.VMEM(child_field.shape, bf16),
+            dma((5, owners, 2)),
+            dma((owners, 2)),
+            dma((5, owners, 2)),
+            dma((owners, 2)),
+            dma((CHUNKS,)),
+            dma((CHUNKS,)),
+            dma((CHUNKS,)),
+            dma((CHUNKS,)),
+            dma((4,)),
+        ],
+        compiler_params=pltpu.CompilerParams(
+            collective_id=0, has_side_effects=True, vmem_limit_bytes=58 * 2**20
+        ),
+    )(*fields, *tables)
+
+
 def local(
     child_field,
     child_list,
@@ -135,14 +459,21 @@
     parent_rows = parent_list.shape[0]
     child_thin = child_field.shape[2]
     parent_thin = parent_ops.shape[2]
-    whole_polar = lax.all_gather(child_field, "angle", axis=2, tiled=True)
-    child_all = lax.all_gather(child_field, "box", axis=0, tiled=True)
     theta = fourier_table(PT, CT, 0.5)
     phi = fourier_table(PP, SUBBOX_HEADINGS, 0.0)
     theta_up = theta.astype(jnp.bfloat16)
     phi_up = phi.T.astype(jnp.bfloat16)
     theta_down = (theta.T * (CT / PT)).astype(jnp.bfloat16)
     phi_down = (phi * (SUBBOX_HEADINGS / PP)).astype(jnp.bfloat16)
+    cos_piece, sin_piece = shift_parts(jnp.arange(PT, dtype=jnp.int32))
+    if (lax.axis_size("box"), lax.axis_size("angle")) == (Z * Y * C, 2):
+        fields = (
+            child_field, child_list, child_op, child_home, child_ops,
+            parent_list, parent_op, parent_home, parent_ops,
+        )
+        return whole(fields, (theta_up, phi_up, theta_down, phi_down, cos_piece, sin_piece))
+    whole_polar = lax.all_gather(child_field, "angle", axis=2, tiled=True)
+    child_all = lax.all_gather(child_field, "box", axis=0, tiled=True)
     up_rows = lax.dynamic_slice_in_dim(theta_up, angle_index * parent_thin, parent_thin, 0)
     stretched = jnp.einsum(
         "ut,rctp->rcup", up_rows, whole_polar, preferred_element_type=jnp.float32
@@ -160,7 +491,6 @@
     )
     down_rows = lax.dynamic_slice_in_dim(theta_down, angle_index * child_thin, child_thin, 0)
     parents = lax.all_gather(parent_far, "angle", axis=2, tiled=True)
-    cos_piece, sin_piece = shift_parts(jnp.arange(PT, dtype=jnp.int32))
     turned = lower_turn(parents, cos_piece, sin_piece)
     narrowed = jnp.einsum(
         "qkcuv,vp->qkcup", turned, phi_down, preferred_element_type=jnp.float32

time: 366 us -> 233 us (0.64)
  waiting for transfers between devices: 294 us -> 0 us
  Pallas kernels: 12.9 us -> 217 us
  other arithmetic: 19.1 us -> 4.23 us
  between operations: 13.3 us -> 0.06 us
  matrix products: 14.4 us -> 1.92 us
    all_gather x4 -> x0, waiting for transfers between devices: 293 us -> none  [the longest x1 126 us: local(): parent_all = lax.all_gather(parent_field, 'box', axis=0, tiled=True)]
    pallas_call x2 -> x1, Pallas kernels: 12.9 us -> 217 us  [whole(): pl.pallas_call(whole_kernel, out_shape=jax.ShapeDtypeStruct(child_field.s...]
    dot_general x2 -> x0, matrix products: 13.7 us -> none  [the longest x1 6.88 us: local(): jnp.einsum('tu,qkcup->qkctp', down_rows, narrowed, preferred_element_type...]
    another operation x2 -> x0, other arithmetic: 5.84 us -> none
    reduce_sum x1 -> x0, other arithmetic: 4.59 us -> none  [lift_sum(): jnp.sum(cos_part * widened[..., 0, :, :] - sin_part * widened[..., 1, :,...]
    unnamed x28 -> x5, local copies, waits for them, and re-layouts: 12 us -> 7.72 us
    cos x2 -> x0, other arithmetic: 3.79 us -> none  [shift_parts(): return (jnp.cos(phase_arg), jnp.sin(phase_arg))]
  transfers between devices with their start and end apart: 4 -> 0, of which waited for: 4 -> 0; matrix products, arithmetic and copies ran while one was open for 2% -> 0% of each run, Pallas kernels for 4% -> 0%
where the time goes in v2:
time: 233 us; the launch traced here: 232 us
  Pallas kernels  217 us (93%)
  local copies, waits for them, and re-layouts  9.18 us (4%)
  other arithmetic  4.23 us (2%)
    pallas_call x1, Pallas kernels, whole(): pl.pallas_call(whole_kernel, out_shape=jax.ShapeDtypeStruct(child_field.s...  217 us
    unnamed x5, local copies, waits for them, and re-layouts  7.72 us

profile of v2, /device:TPU:0, one launch (start us, length us, event | category | flops | bytes accessed | tf_op | source)
XLA Modules:
  0.0 232.4 jit_solution(5718497486114837225)
XLA Ops:
  0.2 0.1 multiply_add_fusion
  0.2 1.4 copy.19.parent_list
  1.6 1.3 copy.20.parent_op
  2.9 1.4 copy.17.child_list
  4.3 1.4 copy.18.child_op
  5.7 0.1 cosine_multiply_fusion.1
  5.8 0.2 fusion.42
  6.0 0.8 fusion.40
  6.8 0.7 copy.21.theta_up
  7.6 0.3 fusion.30
  7.9 0.6 cosine_multiply_fusion
  8.5 1.1 multiply_convert_fusion
  9.6 0.7 copy.16
  10.3 2.8 %multiply_sine_fusion = (f32[4,128,256]{2,1,0:T(8,128)}, f32[4,128,256]{2,1,0:T(8,128)}) fusion(f32[4,256]{1,0:T(4,128)S(1)} %multiply_add_fusion, f32[128]{0:T(128)S(1)} %sine_multiply_fusion.2), kind=kLoop, calls=%fused_computation | loop fusion | flops 131072 | bytes 1053184 | tf_op jit(solution)/shard_map/sin | solution.py:49
  13.1 217.1 %shard_map.91 = bf16[64,2,32,128]{3,2,1,0:T(8,128)(2,1)} custom-call(bf16[64,2,32,128]{3,2,1,0:T(8,128)(2,1)} %child_field.1, s32[64,8]{1,0:T(8,128)} %copy.17.child_list, s32[64,8]{1,0:T(8,128)} %copy.18.child_op, s32[1024]{0:T(1024)} %child_home.1, bf16[40,2,32,128]{3,2,1,0:T(8,128)(2,1)} %child_ops.1, s32[16,8]{1,0:T(8,128)} %copy.19.parent_list, ...), custom_call_target="tpu_custom_call" | custom-call | tf_op jit(solution)/shard_map/pallas_call | solution.py:417
  230.2 2.3 copy.23
  (9 shorter events, 0.1 us)

commit v3 on v2

--- a/solution.py
+++ b/solution.py
@@ -220,10 +220,10 @@
 def translate(lists, op, home, field, padded, r, empty, start, span):
     part = pl.ds(start, span)
     real = imag = None
-    for j in range(lists.shape[1]):
-        box = lists[r, j]
+    for j in range(lists.shape[0]):
+        box = lists[j, r]
         at = home[jnp.maximum(box, 0)]
-        oper = jnp.where(box >= 0, op[r, j], empty)
+        oper = jnp.where(box >= 0, op[j, r], empty)
         a = padded[oper, 0, part, :].astype(jnp.float32)
         b = padded[oper, 1, part, :].astype(jnp.float32)
         c = field[at, 0, part, :].astype(jnp.float32)
@@ -245,7 +245,7 @@
     box, angle = lax.axis_index("box"), lax.axis_index("angle")
     z, y, c = box // (Y * C), (box // C) % Y, box % C
     children, child_thin = child_field.shape[0], child_field.shape[2]
-    parents, parent_thin = parent_list.shape[0], far.shape[3]
+    parents, parent_thin = parent_list.shape[1], far.shape[3]
     kids_rows, group = children // CHUNKS, parents // CHUNKS
     child_empty, parent_empty = child_ops.shape[0], parent_ops.shape[0]
     MESH = pl.DeviceIdType.MESH
@@ -329,12 +329,12 @@
         if i % 2:
             parents_of.first(i // 2)
 
+    children_of.step(1)
     parents_of.step(1)
-    children_of.step(1)
     parents_of.step(2)
+    children_of.step(2)
     parents_of.step(3)
     parents_of.finish()
-    children_of.step(2)
 
     span = min(parent_thin, 4096 // PP)
 
@@ -383,11 +383,10 @@
                 terms[q * KIDS + k, ri] = summed[:, i * SUBBOX_HEADINGS : (i + 1) * SUBBOX_HEADINGS]
         return carry
 
+    children_of.step(3)
     for i in range(CHUNKS):
         back[i].wait_recv()
         lax.fori_loop(i * group, (i + 1) * group, lower, 0)
-
-    children_of.step(3)
     children_of.finish()
 
     def child_row(r, carry):
@@ -406,7 +405,10 @@
 
 
 def whole(fields, tables):
-    child_field, child_list, _, _, child_ops, parent_list, _, _, parent_ops = fields
+    (
+        child_field, child_list, child_op, child_home, child_ops,
+        parent_list, parent_op, parent_home, parent_ops,
+    ) = fields
     owners, angles = lax.axis_size("box"), lax.axis_size("angle")
     parent_shape = (parent_list.shape[0], 2) + parent_ops.shape[2:]
     smem = pl.BlockSpec(memory_space=pltpu.SMEM)
@@ -440,7 +442,10 @@
         compiler_params=pltpu.CompilerParams(
             collective_id=0, has_side_effects=True, vmem_limit_bytes=58 * 2**20
         ),
-    )(*fields, *tables)
+    )(
+        child_field, child_list.T, child_op.T, child_home, child_ops,
+        parent_list.T, parent_op.T, parent_home, parent_ops, *tables,
+    )
 
 
 def local(

time: 233 us -> 215 us (0.923)
  Pallas kernels: 217 us -> 205 us
  local copies, waits for them, and re-layouts: 9.18 us -> 3.72 us
    pallas_call x1, Pallas kernels: 217 us -> 205 us  [whole(): pl.pallas_call(whole_kernel, out_shape=jax.ShapeDtypeStruct(child_field.s...]
    unnamed x5 -> x1, local copies, waits for them, and re-layouts: 7.72 us -> 2.26 us
where the time goes in v3:
time: 215 us
  Pallas kernels  205 us (95%)
  other arithmetic  4.23 us (2%)
  local copies, waits for them, and re-layouts  3.72 us (2%)
    pallas_call x1, Pallas kernels, whole(): pl.pallas_call(whole_kernel, out_shape=jax.ShapeDtypeStruct(child_field.s...  205 us

profile of v3, /device:TPU:0, one launch (start us, length us, event | category | flops | bytes accessed | tf_op | source)
XLA Modules:
  0.0 214.7 jit_solution(6677959782627590703)
XLA Ops:
  0.2 0.1 multiply_add_fusion
  0.2 0.1 cosine_multiply_fusion.1
  0.3 0.2 fusion.42
  0.6 0.8 fusion.40
  1.4 0.7 copy.13.theta_up
  2.1 0.3 fusion.30
  2.5 0.6 cosine_multiply_fusion
  3.1 1.1 multiply_convert_fusion
  4.1 0.7 copy.12
  4.9 2.8 %multiply_sine_fusion = (f32[4,128,256]{2,1,0:T(8,128)}, f32[4,128,256]{2,1,0:T(8,128)}) fusion(f32[4,256]{1,0:T(4,128)S(1)} %multiply_add_fusion, f32[128]{0:T(128)S(1)} %sine_multiply_fusion.2), kind=kLoop, calls=%fused_computation | loop fusion | flops 131072 | bytes 1053184 | tf_op jit(solution)/shard_map/sin | solution.py:49
  7.7 204.8 %shard_map.91 = bf16[64,2,32,128]{3,2,1,0:T(8,128)(2,1)} custom-call(bf16[64,2,32,128]{3,2,1,0:T(8,128)(2,1)} %child_field.1, s32[8,64]{1,0:T(8,128)} %bitcast.10, s32[8,64]{1,0:T(8,128)} %bitcast.11, s32[1024]{0:T(1024)} %child_home.1, bf16[40,2,32,128]{3,2,1,0:T(8,128)(2,1)} %child_ops.1, s32[8,16]{1,0:T(8,128)} %bitcast.12, s32[8,16]{1,0:T(8,128)} %bitcast.13, ...), custom_call_target="tpu_custom_call" | custom-call | tf_op jit(solution)/shard_map/pallas_call | solution.py:419
  212.4 2.3 %copy.15 = bf16[64,2,32,128]{3,2,1,0:T(8,128)(2,1)} copy(bf16[64,2,32,128]{3,2,1,0:T(8,128)(2,1)} %shard_map.91) | data formatting | bytes 2097152
  (9 shorter events, 0.1 us)
